TPU v7x, 512 devices: a whole 4x4x16 slice. The times are simulated.
512 devices in a mesh: tm: 8 (over y_hi, x), chan: 64 (over y_lo, z, core).
Axes of the slice: x: 4, y: 4 (y_hi: 2, y_lo: 2; y = y_hi * 2 + y_lo), z: 16, core: 2. Of those that a mesh axis runs over, the one named last changes fastest.
Arguments:
- samples: bfloat16 [2048, 262144], P('chan', 'tm'), may hold values from -144 to 144
- input_map: int32 [2048], replicated, may hold values from 0 to 2047, each once
Outputs:
- visibilities: bfloat16 [64, 2, 2048, 2048], P('chan', None, 'tm')
Inputs may be any that keep to these rules, and one draw needn't show every extreme that they name: `input_map`: each of 0 .. 2047 appears once.
All inputs are finite; a program needn't handle non-finite values.
Results may differ from a plain program's by a relative error of at most 0.0069.
Values may be sent and summed in bfloat16 or wider, within the bound.
A program may use at most 64 MiB of HBM per device.

v0:
```python
import math

import jax
import jax.numpy as jnp
from jax import lax
from jax.sharding import PartitionSpec as P

NFFT = 8192
TAPS = 4
CH_DEV = 1


def from_behind(block, axis, distance):
    devices = range(lax.axis_size(axis))
    route = [(i - distance, i) for i in devices if i - distance in devices]
    return lax.ppermute(block, axis, route)


def window_table(frame_len, tap_count, first_channel, channel_count):
    sample_pos = jnp.arange(tap_count * frame_len, dtype=jnp.float32)
    offset = (sample_pos + 0.5 - 0.5 * tap_count * frame_len) / frame_len
    taper = 0.5 - 0.5 * jnp.cos(2.0 * jnp.pi * (sample_pos + 0.5) / (tap_count * frame_len))
    weights = jnp.sinc(offset) * taper / (128.0 * math.sqrt(frame_len))
    per_tap = weights.reshape(tap_count, frame_len).T
    within = jnp.arange(frame_len, dtype=jnp.int32)
    channel_ids = first_channel + jnp.arange(channel_count, dtype=jnp.int32)
    phase = within[:, None] * channel_ids[None, :] % frame_len
    theta = 2.0 * jnp.pi * phase.astype(jnp.float32) / frame_len
    cosine = per_tap[:, :, None] * jnp.cos(theta)[:, None, :]
    sine = -per_tap[:, :, None] * jnp.sin(theta)[:, None, :]
    return jnp.stack([cosine, sine], axis=2).astype(jnp.bfloat16)


def shards(samples, input_map):
    inputs_here, span = samples.shape
    spectra_dev = span // NFFT
    channel_total = CH_DEV * lax.axis_size("chan")
    first_channel = (NFFT // 2 - channel_total) // 2
    twiddle = window_table(NFFT, TAPS, first_channel, channel_total)
    frame_count = min(spectra_dev, TAPS - 1)
    segment = samples[:, (spectra_dev - frame_count) * NFFT :]
    segments = [from_behind(segment, "tm", 1)]
    extended = jnp.concatenate(segments + [samples], axis=1)
    extended = extended.reshape(inputs_here, spectra_dev + TAPS - 1, NFFT)
    accum = jnp.zeros((spectra_dev, 2, channel_total, inputs_here), jnp.float32)
    for tap_index in range(TAPS):
        accum = accum + jnp.einsum(
            "afn,nrk->frka",
            extended[:, tap_index : tap_index + spectra_dev],
            twiddle[:, tap_index],
            preferred_element_type=jnp.float32,
        )
    spectra = accum.astype(jnp.bfloat16)
    turned = lax.all_to_all(spectra, "chan", split_axis=2, concat_axis=3, tiled=True)
    gathered = lax.all_gather(turned, "tm", axis=0, tiled=True)
    ordered = jnp.take(gathered, input_map, axis=3)
    signal_total = ordered.shape[3]
    row_count = signal_total // lax.axis_size("tm")
    row_start = lax.axis_index("tm") * row_count
    own_rows = lax.dynamic_slice_in_dim(ordered, row_start, row_count, 3)
    flipped = jnp.stack([own_rows[:, 1], -own_rows[:, 0]], axis=1)
    paired = jnp.concatenate([own_rows, flipped], axis=3)
    products = jnp.einsum("srcq,srcn->cqn", paired, ordered, preferred_element_type=jnp.float32)
    products = products.reshape(products.shape[0], 2, row_count, signal_total)
    return (products / gathered.shape[0]).astype(jnp.bfloat16)


def solution(mesh):
    in_specs = (P("chan", "tm"), P())
    out_specs = P("chan", None, "tm", None)
    return jax.shard_map(shards, mesh=mesh, in_specs=in_specs, out_specs=out_specs, check_vma=False)
```

profile of v0, /device:TPU:16, one launch (start us, length us, event | category | flops | bytes accessed | tf_op | source)
XLA Modules:
  0.0 150.7 jit_solution(7892422122136973002)
XLA Ops:
  0.0 2.7 %slice.34 = bf16[32,24576]{1,0:T(8,128)(2,1)} slice(bf16[32,32768]{1,0:T(8,128)(2,1)} %param.2), slice={[0:32], [8192:32768]} | slice | bytes 3145728 | tf_op jit(solution)/shard_map/slice | solution.py:41
  2.7 3.4 %collective-permute-start = (bf16[32,24576]{1,0:T(8,128)(2,1)}, bf16[32,24576]{1,0:T(8,128)(2,1)}, u32[]{:S(2)}, u32[]{:S(2)}) collective-permute-start(bf16[32,24576]{1,0:T(8,128)(2,1)} %slice.34), channel_id=1, source_target_pairs={{0,64},{64,128},{128,192},{192,256},{256,320},{320,384},{384,448},... | collective-permute-start | bytes 4718600 | tf_op jit(solution)/shard_map/ppermute | solution.py:16
  6.1 1.3 fusion.49
  7.3 1.3 fusion.58
  8.6 0.0 copy-start.3
  8.6 9.8 %fusion.40 = (f32[8192,64]{0,1:T(8,128)S(1)}, f32[8192,64]{0,1:T(8,128)}) fusion(s32[64]{0:T(128)S(1)} %iota_add_fusion), kind=kLoop, calls=%fused_computation.45 | loop fusion | flops 7340032 | bytes 4194560 | tf_op jit(solution)/shard_map/cos | solution.py:29
  18.4 0.0 copy-done.3
  18.4 0.1 dynamic-slice
  18.5 0.0 copy-start.2
  18.5 5.4 %multiply_convert_fusion = (bf16[8192,4,1,64]{0,3,2,1:T(8,128)(2,1)}, bf16[8192,4,1,64]{0,3,2,1:T(8,128)(2,1)}) fusion(f32[8192,64]{0,1:T(8,128)} %get-tuple-element.12, f32[8192,4]{0,1:T(4,128)S(1)} %fusion.58, f32[8192,64]{0,1:T(8,128)S(1)} %get-tuple-element.11, f32[8192,4]{0,1:T(4,128)S(1)} %fusion.49), kind=kLoop, calls=%fused_computation.7 | loop fusion | flops 8388608 | bytes 12845056 | tf_op jit(solution)/shard_map/convert.1
  23.9 20.7 %collective-permute-done = bf16[32,24576]{1,0:T(8,128)(2,1)} collective-permute-done((bf16[32,24576]{1,0:T(8,128)(2,1)}, bf16[32,24576]{1,0:T(8,128)(2,1)}, u32[]{:S(2)}, u32[]{:S(2)}) %collective-permute-start) | collective-permute-done | bytes 1572896 | tf_op jit(solution)/shard_map/ppermute | solution.py:16
  44.6 0.0 copy-done.2
  44.6 3.4 %pad_maximum_fusion = bf16[32,57344]{1,0:T(8,128)(2,1)} fusion(bf16[32,32768]{1,0:T(8,128)(2,1)S(1)} %copy-done.2, bf16[32,24576]{1,0:T(8,128)(2,1)} %collective-permute-done), kind=kLoop, calls=%fused_computation.11 | loop fusion | flops 7340032 | bytes 7340032 | tf_op jit(solution)/shard_map/concatenate | solution.py:43
  48.0 7.9 %reshape.99 = bf16[32,7,8192]{2,1,0:T(8,128)(2,1)} reshape(bf16[32,57344]{1,0:T(8,128)(2,1)} %pad_maximum_fusion) | data formatting | bytes 7340032 | tf_op jit(solution)/shard_map/reshape | solution.py:44
  56.0 0.0 copy-start
  56.0 0.0 copy-start.1
  56.0 11.2 %fusion.65 = (bf16[32,4,8192]{2,1,0:T(4,128)(2,1)S(1)}, bf16[32,4,8192]{2,1,0:T(4,128)(2,1)S(1)}, bf16[32,4,8192]{2,1,0:T(4,128)(2,1)S(1)}, bf16[32,4,8192]{2,1,0:T(4,128)(2,1)S(1)}) fusion(bf16[32,7,8192]{2,1,0:T(8,128)(2,1)} %reshape.99), kind=kLoop, calls=%fused_computation.89 | loop fusion | bytes 16777216 | tf_op jit(solution)/shard_map/slice | solution.py:49
  67.2 0.0 copy-done
  67.2 0.0 copy-done.1
  67.3 1.7 %fusion.16 = f32[2,64,32,4]{1,2,3,0:T(8,128)S(1)} fusion(bf16[32,4,8192]{2,1,0:T(4,128)(2,1)S(1)} %get-tuple-element.7, bf16[8192,4,1,64]{0,3,2,1:T(8,128)(2,1)S(1)} %copy-done.1, bf16[8192,4,1,64]{0,3,2,1:T(8,128)(2,1)S(1)} %copy-done), kind=kOutput, calls=%fused_computation.33 | convolution fusion | flops 272629760 | bytes 10551296 | tf_op jit(solution)/shard_map/afn,nrk->frka/dot_general | solution.py:47
  69.0 1.7 %fusion.15 = f32[2,64,32,4]{1,2,3,0:T(8,128)S(1)} fusion(bf16[32,4,8192]{2,1,0:T(4,128)(2,1)S(1)} %get-tuple-element.6, bf16[8192,4,1,64]{0,3,2,1:T(8,128)(2,1)S(1)} %copy-done.1, bf16[8192,4,1,64]{0,3,2,1:T(8,128)(2,1)S(1)} %copy-done), kind=kOutput, calls=%fused_computation.31 | convolution fusion | flops 272629760 | bytes 10551296 | tf_op jit(solution)/shard_map/afn,nrk->frka/dot_general | solution.py:47
  70.7 1.7 %fusion.12 = f32[2,64,32,4]{1,2,3,0:T(8,128)S(1)} fusion(bf16[8192,4,1,64]{0,3,2,1:T(8,128)(2,1)S(1)} %copy-done, bf16[8192,4,1,64]{0,3,2,1:T(8,128)(2,1)S(1)} %copy-done.1, bf16[32,4,8192]{2,1,0:T(4,128)(2,1)S(1)} %get-tuple-element.8), kind=kOutput, calls=%fused_computation.27 | convolution fusion | flops 272629760 | bytes 10551296 | tf_op jit(solution)/shard_map/afn,nrk->frka/dot_general | solution.py:47
  72.4 1.7 %fusion.36 = bf16[4,2,64,32]{2,3,0,1:T(8,128)(2,1)S(1)} fusion(f32[2,64,32,4]{1,2,3,0:T(8,128)S(1)} %fusion.12, f32[2,64,32,4]{1,2,3,0:T(8,128)S(1)} %fusion.15, f32[2,64,32,4]{1,2,3,0:T(8,128)S(1)} %fusion.16, bf16[32,4,8192]{2,1,0:T(4,128)(2,1)S(1)} %get-tuple-element.5, bf16[8192,4,1,64]{0,3,2,1:T(8,128)(2,1)S(1)} %copy-done.1, ...), kind=kOutput, calls=%fused_computation.43 | convolution fusion | flops 272695296 | bytes 10715136 | tf_op jit(solution)/shard_map/afn,nrk->frka/dot_general | solution.py:47
  74.1 0.1 copy.31
  74.3 0.7 reshape.123
  75.0 16.8 %all-to-all-start = ((bf16[64,2,128]{2,1,0:T(2,128)(2,1)}), bf16[64,2,128]{2,1,0:T(2,128)(2,1)S(1)}, u32[]{:S(2)}, u32[]{:S(2)}) async-start(bf16[64,2,128]{2,1,0:T(2,128)(2,1)} %reshape.123), calls=%async_computation | async-start | bytes 65536 | tf_op jit(solution)/shard_map/all_to_all | solution.py:54
  91.9 13.3 %all-to-all-done = bf16[64,2,128]{2,1,0:T(2,128)(2,1)S(1)} async-done(((bf16[64,2,128]{2,1,0:T(2,128)(2,1)}), bf16[64,2,128]{2,1,0:T(2,128)(2,1)S(1)}, u32[]{:S(2)}, u32[]{:S(2)}) %all-to-all-start) | async-done | bytes 32800 | tf_op jit(solution)/shard_map/all_to_all | solution.py:54
  105.2 0.1 reshape.124
  105.3 0.2 all_to_all.10
  105.5 34.5 %all_gather.3 = bf16[32,2,1,2048]{3,1,2,0:T(2,128)(2,1)S(1)} all-gather(bf16[4,2,1,2048]{3,1,2,0:T(2,128)(2,1)S(1)} %bitcast.94), channel_id=1, replica_groups=mesh['tm'=8,'chan'=64] {'tm'}, dimensions={0}, use_global_device_ids=true | all-gather | bytes 294912 | tf_op jit(solution)/shard_map/all_gather | solution.py:55
  140.0 0.8 copy.35
  140.8 7.1 %gather_fusion = bf16[2048,32,2]{1,2,0:T(2,128)(2,1)S(1)} fusion(bf16[32,2,2048]{0,1,2:T(2,128)(2,1)S(1)} %copy.35, s32[2048]{0:T(1024)S(1)} %fusion.59), kind=kCustom, calls=%fused_computation | custom fusion | bytes 532480 | tf_op jit(solution)/shard_map/jit(_take)/gather | solution.py:56
  147.9 0.7 copy.36
  148.6 2.0 %fusion.1 = bf16[1,2,256,2048]{3,2,1,0:T(8,128)(2,1)} fusion(bf16[2048,32,2]{0,1,2:T(8,128)(2,1)S(1)} %copy.36, pred[2048]{0:T(1024)(128)(4,1)S(1)} %compare_and_fusion, bf16[2,4,2,8,256]{4,3,2,1,0:T(8,128)(2,1)S(1)} %bitcast.95), kind=kOutput, calls=%fused_computation.15 | convolution fusion | flops 136445952 | bytes 2426880 | tf_op jit(solution)/shard_map/srcq,srcn->cqn/dot_general | solution.py:63
  (7 shorter events, 0.1 us)
Async XLA Ops:
  2.7 41.9 %collective-permute-start = (bf16[32,24576]{1,0:T(8,128)(2,1)}, bf16[32,24576]{1,0:T(8,128)(2,1)}, u32[]{:S(2)}, u32[]{:S(2)}) collective-permute-start(bf16[32,24576]{1,0:T(8,128)(2,1)} %slice.34), channel_id=1, source_target_pairs={{0,64},{64,128},{128,192},{192,256},{256,320},{320,384},{384,448},... | collective-permute-start | bytes 4718600 | tf_op jit(solution)/shard_map/ppermute | solution.py:16
  8.6 9.8 %copy-start.3 = (s32[2048]{0:T(1024)S(1)}, s32[2048]{0:T(1024)}, u32[]{:S(2)}) copy-start(s32[2048]{0:T(1024)} %param.3) | copy-start | bytes 24580
  18.5 26.1 %copy-start.2 = (bf16[32,32768]{1,0:T(8,128)(2,1)S(1)}, bf16[32,32768]{1,0:T(8,128)(2,1)}, u32[]{:S(2)}) copy-start(bf16[32,32768]{1,0:T(8,128)(2,1)} %param.2) | copy-start | bytes 6291460
  56.0 11.3 %copy-start = (bf16[8192,4,1,64]{0,3,2,1:T(8,128)(2,1)S(1)}, bf16[8192,4,1,64]{0,3,2,1:T(8,128)(2,1)}, u32[]{:S(2)}) copy-start(bf16[8192,4,1,64]{0,3,2,1:T(8,128)(2,1)} %get-tuple-element.13) | copy-start | bytes 12582916
  56.0 11.3 %copy-start.1 = (bf16[8192,4,1,64]{0,3,2,1:T(8,128)(2,1)S(1)}, bf16[8192,4,1,64]{0,3,2,1:T(8,128)(2,1)}, u32[]{:S(2)}) copy-start(bf16[8192,4,1,64]{0,3,2,1:T(8,128)(2,1)} %get-tuple-element.14) | copy-start | bytes 12582916
  75.0 30.1 %all-to-all-start = ((bf16[64,2,128]{2,1,0:T(2,128)(2,1)}), bf16[64,2,128]{2,1,0:T(2,128)(2,1)S(1)}, u32[]{:S(2)}, u32[]{:S(2)}) async-start(bf16[64,2,128]{2,1,0:T(2,128)(2,1)} %reshape.123), calls=%async_computation | async-start | bytes 65536 | tf_op jit(solution)/shard_map/all_to_all | solution.py:54
where the time goes:
time: 151 us
  blocking collectives  34.5 us (23%)
  waiting for transfers between devices  34 us (23%)
  local copies, waits for them, and re-layouts  31.7 us (21%)
  other arithmetic  21.2 us (14%)
  starting transfers between devices  20.2 us (13%)
  matrix products  8.9 us (6%)
    all_gather x1, blocking collectives, shards(): gathered = lax.all_gather(turned, 'tm', axis=0, tiled=True)  34.5 us
    ppermute x1, waiting for transfers between devices, from_behind(): return lax.ppermute(block, axis, route)  20.7 us
    all_to_all x1, starting transfers between devices, shards(): lax.all_to_all(spectra, 'chan', split_axis=2, concat_axis=3, tiled=True)  16.8 us
    all_to_all x1, waiting for transfers between devices, shards(): lax.all_to_all(spectra, 'chan', split_axis=2, concat_axis=3, tiled=True)  13.3 us
    slice x1, local copies, waits for them, and re-layouts, shards(): extended[:, tap_index:tap_index + spectra_dev]  11.2 us
    cos x1, other arithmetic, window_table(): cosine = per_tap[:, :, None] * jnp.cos(theta)[:, None, :]  9.8 us
    reshape x1, local copies, waits for them, and re-layouts, shards(): extended = extended.reshape(inputs_here, spectra_dev + TAPS - 1, NFFT)  7.95 us
    gather x2, local copies, waits for them, and re-layouts, shards(): ordered = jnp.take(gathered, input_map, axis=3)  7.73 us
  transfers between devices with their start and end apart: 2, of which 2 were waited for; matrix products, arithmetic and copies ran while one was open for 12% of the time, Pallas kernels for 0%

commit v1 on v0

v1 whole, which is shorter than its diff:
```python
import functools
import math

import jax
import jax.numpy as jnp
import ml_dtypes
import numpy as np
from jax import lax
from jax.experimental import pallas as pl
from jax.experimental.pallas import tpu as pltpu
from jax.sharding import PartitionSpec as P

NFFT = 8192
TAPS = 4
CHUNK = 1024
PARTS = 2
GROUP = 4
VMEM_BYTES = 61 * 1024 * 1024
GRAM_BYTES = 24 * 1024 * 1024
MESH = pl.DeviceIdType.MESH


def twiddle_table(channel_total):
    first_channel = (NFFT // 2 - channel_total) // 2
    m = np.arange(TAPS * NFFT, dtype=np.float64)
    offset = (m + 0.5 - 0.5 * TAPS * NFFT) / NFFT
    taper = 0.5 - 0.5 * np.cos(2.0 * np.pi * (m + 0.5) / (TAPS * NFFT))
    coefficient = np.sinc(offset) * taper / (128.0 * math.sqrt(NFFT))
    coefficient = coefficient.astype(np.float32).reshape(TAPS, NFFT)
    n = np.arange(NFFT, dtype=np.int64)
    channels = first_channel + np.arange(channel_total, dtype=np.int64)
    theta = 2.0 * np.pi * ((channels[:, None] * n[None, :]) % NFFT) / NFFT
    wave = np.stack([np.cos(theta), -np.sin(theta)], axis=1).astype(np.float32)
    wave = wave.reshape(2, channel_total // 4, 2, 2, NFFT)
    wave = wave.transpose(0, 2, 3, 1, 4).reshape(2 * channel_total, NFFT)
    table = (coefficient[:, None, :] * wave[None]).reshape(-1, NFFT)
    return np.ascontiguousarray(table.T).astype(ml_dtypes.bfloat16)


def turn_kernel(
    n_tm, n_z, x_hbm, tw_hbm, map_hbm, out_ref,
    tw_v, map_ref, xs, acc, own, halo, own_in, halo_in, tiles32, tiles, ring, low_hot,
    tw_sem, map_sem, x_sem, s1_send, s1_recv, h_send, h_recv, z_send, z_recv, t_send, t_recv,
):
    span = NFFT // PARTS
    chunks = span // CHUNK
    half = 2 * 2 * 2 * n_z
    tm = lax.axis_index("tm")
    chan = lax.axis_index("chan")
    y_lo = chan // (2 * n_z)
    z = (chan // 2) % n_z
    core = chan % 2
    group = y_lo * 2 + core

    def chan_of(g, z_at):
        return (g // 2) * (2 * n_z) + z_at * 2 + g % 2

    def load_frames(part):
        return [
            pltpu.make_async_copy(
                x_hbm.at[:, pl.ds(f * NFFT + part * span, span)],
                xs.at[part, f],
                x_sem.at[part, f],
            )
            for f in range(TAPS)
        ]

    def load_table(c):
        at = pl.ds(pl.multiple_of(c * CHUNK, CHUNK), CHUNK)
        return pltpu.make_async_copy(tw_hbm.at[at], tw_v.at[at], tw_sem.at[c])

    for part in range(PARTS):
        for copy in load_frames(part):
            copy.start()
        for c in range(part * chunks, (part + 1) * chunks):
            load_table(c).start()
    signal_map = pltpu.make_async_copy(map_hbm, map_ref, map_sem)
    signal_map.start()

    barrier = pltpu.get_barrier_semaphore()

    def greet(tm_at, chan_at):
        pl.semaphore_signal(
            barrier, inc=1, device_id={"tm": tm_at, "chan": chan_at}, device_id_type=MESH
        )

    next_tm = (tm + 1) % n_tm
    prev_tm = (tm + n_tm - 1) % n_tm
    for e in range(1, GROUP):
        greet(tm, chan_of((group + e) % GROUP, z))
    for e in range(GROUP):
        greet(prev_tm, chan_of((group + e) % GROUP, z))
    for d in range(1, n_z):
        greet(tm, chan_of(group, (z + d) % n_z))
    for e in range(1, n_tm):
        greet((tm + e) % n_tm, chan)

    for part in range(PARTS):
        for copy in load_frames(part):
            copy.wait()
        for i in range(chunks):
            c = part * chunks + i
            load_table(c).wait()
            frames = xs[part, :, :, i * CHUNK : (i + 1) * CHUNK].reshape(TAPS * 32, CHUNK)
            table = tw_v[c * CHUNK : (c + 1) * CHUNK, :]
            product = jnp.dot(frames, table, preferred_element_type=jnp.float32)
            acc[...] = product if c == 0 else acc[...] + product

    def tap_sum(s, taps):
        return sum(
            acc[(s + t) % TAPS * 32 : ((s + t) % TAPS + 1) * 32, t * half : (t + 1) * half]
            for t in taps
        )

    here = [tap_sum(s + 1, range(TAPS - 1 - s, TAPS)) for s in range(TAPS)]
    later = [tap_sum(s + 1, range(TAPS - 1 - s)) for s in range(TAPS - 1)]
    later.append(jnp.zeros_like(later[0]))
    here = jnp.concatenate(here, axis=0).T
    later = jnp.concatenate(later, axis=0).T
    own[...] = here.reshape(GROUP, half // GROUP, 128)
    halo[...] = later.astype(jnp.bfloat16).reshape(GROUP, half // GROUP, 128)

    pl.semaphore_wait(barrier, (GROUP - 1) + GROUP + (n_z - 1) + (n_tm - 1))

    sends = []
    recvs = []
    for e in range(GROUP):
        to = (group + e) % GROUP
        copy = pltpu.make_async_remote_copy(
            src_ref=halo.at[to], dst_ref=halo_in.at[group],
            send_sem=h_send.at[e], recv_sem=h_recv.at[e],
            device_id={"tm": next_tm, "chan": chan_of(to, z)}, device_id_type=MESH,
        )
        copy.start()
        sends.append(copy)
        recvs.append(copy)
    for e in range(1, GROUP):
        to = (group + e) % GROUP
        copy = pltpu.make_async_remote_copy(
            src_ref=own.at[to], dst_ref=own_in.at[group],
            send_sem=s1_send.at[e], recv_sem=s1_recv.at[e],
            device_id={"tm": tm, "chan": chan_of(to, z)}, device_id_type=MESH,
        )
        copy.start()
        sends.append(copy)
        recvs.append(copy)
    own_in[group] = own[group]

    signal_map.wait()
    source = map_ref[...]
    source_z = (source // 64) % n_z
    low_of = (source_z % 2) * 128 + (source // (64 * n_z)) * 64 + source % 64
    pair_of = source_z // 2
    low_row = lax.broadcasted_iota(jnp.int32, (256, 1), 0)
    low_hot[...] = jnp.where(low_row == low_of, 1.0, 0.0).astype(jnp.bfloat16)

    for copy in recvs:
        copy.wait_recv()

    block = lax.broadcasted_iota(jnp.int32, (half // GROUP, 128), 1) // 32
    whole = []
    for g in range(GROUP):
        whole.append(own_in[g] + jnp.where(tm > 0, halo_in[g].astype(jnp.float32), 0.0))
    for s in range(TAPS):
        turned = whole[s]
        for g in range(GROUP):
            if g != s:
                turned = jnp.where(
                    block == g, pltpu.roll(whole[g], ((g - s) % GROUP) * 32, 1), turned
                )
        for r in range(2):
            tiles32[pl.ds(r * TAPS + s, n_z, stride=8), :] = turned[r * n_z : (r + 1) * n_z, :]
    tiles[...] = tiles32[...].reshape(n_z, 8, 128).astype(jnp.bfloat16)

    recvs = []
    for d in sorted(range(1, n_z), key=lambda d: abs(d - n_z // 2)):
        to = (z + d) % n_z
        copy = pltpu.make_async_remote_copy(
            src_ref=tiles.at[to], dst_ref=ring.at[z],
            send_sem=z_send.at[d], recv_sem=z_recv.at[d],
            device_id={"tm": tm, "chan": chan_of(group, to)}, device_id_type=MESH,
        )
        copy.start()
        sends.append(copy)
        recvs.append(copy)
    ring[z] = tiles[z]
    for copy in recvs:
        copy.wait_recv()

    n_pair = n_z // 2
    pairs = ring[...].astype(jnp.float32).reshape(n_pair, 2, 8, 128)
    pairs = jnp.concatenate([pairs[:, 0], pairs[:, 1]], axis=-1)
    pairs = pairs.reshape(n_pair * 8, 256).astype(jnp.bfloat16)
    picked = jnp.dot(pairs, low_hot[...], preferred_element_type=jnp.float32)
    ordered = jnp.zeros((8, n_z * 128), jnp.float32)
    for pair in range(n_pair):
        ordered = ordered + jnp.where(pair_of == pair, picked[pair * 8 : (pair + 1) * 8], 0.0)
    out_ref[tm] = ordered.astype(jnp.bfloat16)

    recvs = []
    for e in sorted(range(1, n_tm), key=lambda e: abs(e - n_tm // 2)):
        copy = pltpu.make_async_remote_copy(
            src_ref=out_ref.at[tm], dst_ref=out_ref.at[tm],
            send_sem=t_send.at[e], recv_sem=t_recv.at[e],
            device_id={"tm": (tm + e) % n_tm, "chan": chan}, device_id_type=MESH,
        )
        copy.start()
        sends.append(copy)
        recvs.append(copy)
    for copy in recvs:
        copy.wait_recv()

    for copy in sends:
        copy.wait_send()


def gram_kernel(n_tm, x_ref, out_hbm, left, blocks, out_sem):
    n_block, _, rows, width = blocks.shape

    def packed(x):
        return x.astype(jnp.float32).reshape(n_tm * 8, x.shape[-1]).astype(jnp.bfloat16)

    start = pl.multiple_of(lax.axis_index("tm") * rows, rows)
    mine = x_ref[:, :, pl.ds(start, rows)].astype(jnp.float32)
    row = lax.broadcasted_iota(jnp.int32, mine.shape, 1)
    other = pltpu.roll(mine, 4, 1)
    flipped = jnp.where(row < 4, other, -other)
    left[:rows, :] = mine.reshape(n_tm * 8, rows).T.astype(jnp.bfloat16)
    left[rows:, :] = flipped.reshape(n_tm * 8, rows).T.astype(jnp.bfloat16)
    copies = []
    for j in range(n_block):
        right = packed(x_ref[:, :, j * width : (j + 1) * width])
        products = jnp.dot(left[...], right, preferred_element_type=jnp.float32)
        products = products * (1.0 / (4 * n_tm))
        blocks[j] = products.reshape(2, rows, width).astype(jnp.bfloat16)
        copy = pltpu.make_async_copy(
            blocks.at[j], out_hbm.at[0, :, :, pl.ds(j * width, width)], out_sem.at[j]
        )
        copy.start()
        copies.append(copy)
    for copy in copies:
        copy.wait()


def shards(n_tm, n_chan, table, samples, input_map):
    n_z = n_chan // 4
    signals = 32 * n_chan
    half = 2 * n_chan
    f32, bf16 = jnp.float32, jnp.bfloat16
    dma = pltpu.SemaphoreType.DMA
    ordered = pl.pallas_call(
        functools.partial(turn_kernel, n_tm, n_z),
        out_shape=pltpu.VMEM((n_tm, 8, signals), bf16),
        in_specs=[
            pl.BlockSpec(memory_space=pltpu.HBM),
            pl.BlockSpec(memory_space=pltpu.HBM),
            pl.BlockSpec(memory_space=pltpu.HBM),
        ],
        out_specs=pl.BlockSpec(memory_space=pltpu.VMEM),
        scratch_shapes=[
            pltpu.VMEM((NFFT, TAPS * half), bf16),
            pltpu.VMEM((1, signals), jnp.int32),
            pltpu.VMEM((PARTS, TAPS, 32, NFFT // PARTS), bf16),
            pltpu.VMEM((TAPS * 32, TAPS * half), f32),
            pltpu.VMEM((GROUP, half // GROUP, 128), f32),
            pltpu.VMEM((GROUP, half // GROUP, 128), bf16),
            pltpu.VMEM((GROUP, half // GROUP, 128), f32),
            pltpu.VMEM((GROUP, half // GROUP, 128), bf16),
            pltpu.VMEM((n_z * 8, 128), f32),
            pltpu.VMEM((n_z, 8, 128), bf16),
            pltpu.VMEM((n_z, 8, 128), bf16),
            pltpu.VMEM((256, signals), bf16),
            dma((NFFT // CHUNK,)),
            dma,
            dma((PARTS, TAPS)),
            dma((GROUP,)),
            dma((GROUP,)),
            dma((GROUP,)),
            dma((GROUP,)),
            dma((n_z,)),
            dma((n_z,)),
            dma((n_tm,)),
            dma((n_tm,)),
        ],
        compiler_params=pltpu.CompilerParams(
            collective_id=0, has_side_effects=True, vmem_limit_bytes=VMEM_BYTES
        ),
        name="turn",
    )(samples, jnp.asarray(table), input_map.reshape(1, signals))
    rows = signals // n_tm
    width = min(256, signals)
    n_block = signals // width
    return pl.pallas_call(
        functools.partial(gram_kernel, n_tm),
        out_shape=jax.ShapeDtypeStruct((1, 2, rows, signals), bf16),
        in_specs=[pl.BlockSpec(memory_space=pltpu.VMEM)],
        out_specs=pl.BlockSpec(memory_space=pl.ANY),
        scratch_shapes=[
            pltpu.VMEM((2 * rows, n_tm * 8), bf16),
            pltpu.VMEM((n_block, 2, rows, width), bf16),
            dma((n_block,)),
        ],
        compiler_params=pltpu.CompilerParams(vmem_limit_bytes=GRAM_BYTES),
        name="gram",
    )(ordered)


def solution(mesh):
    n_tm, n_chan = mesh.shape["tm"], mesh.shape["chan"]
    body = functools.partial(shards, n_tm, n_chan, twiddle_table(n_chan))
    in_specs = (P("chan", "tm"), P())
    out_specs = P("chan", None, "tm", None)
    return jax.shard_map(body, mesh=mesh, in_specs=in_specs, out_specs=out_specs, check_vma=False)
```

time: 151 us -> 34.9 us (0.23)
  the two profiles are of different devices: /device:TPU:16 before, /device:TPU:1 now
where the time goes in v1:
time: 34.9 us; the launch traced here: 34.8 us
  Pallas kernels  34.8 us (100%)
    pallas_call x1, Pallas kernels, shards(): pl.pallas_call(functools.partial(turn_kernel, n_tm, n_z), out_shape=pltpu...  33 us
    pallas_call x1, Pallas kernels, shards(): pl.pallas_call(functools.partial(gram_kernel, n_tm), out_shape=jax.ShapeD...  1.75 us

profile of v1, /device:TPU:1, one launch (start us, length us, event | category | flops | bytes accessed | tf_op | source)
XLA Modules:
  0.0 34.8 jit_solution(12109875735711124341)
XLA Ops:
  0.0 33.0 %turn.1.x_ref = bf16[8,8,2048]{2,1,0:T(8,128)(2,1)S(1)} custom-call(bf16[32,32768]{1,0:T(8,128)(2,1)} %x_hbm.1, bf16[8192,512]{1,0:T(8,128)(2,1)} %constant.2.clone.tw_hbm, s32[1,2048]{1,0:T(1,128)} %bitcast.1), custom_call_target="tpu_custom_call" | custom-call | tf_op jit(solution)/shard_map/turn/pallas_call | solution.py:251
  33.0 1.7 %gram.1 = bf16[1,2,256,2048]{3,2,1,0:T(8,128)(2,1)} custom-call(bf16[8,8,2048]{2,1,0:T(8,128)(2,1)S(1)} %turn.1.x_ref), custom_call_target="tpu_custom_call" | custom-call | tf_op jit(solution)/shard_map/gram/pallas_call | solution.py:293

commit v2 on v1

--- a/solution.py
+++ b/solution.py
@@ -12,8 +12,9 @@
 
 NFFT = 8192
 TAPS = 4
-CHUNK = 1024
-PARTS = 2
+PARTS = 4
+CHUNKS = (512, 512, 1024, 1024, 1024, 1024, 1024, 1024, 512, 512)
+STARTS = tuple(sum(CHUNKS[:c]) for c in range(len(CHUNKS)))
 GROUP = 4
 VMEM_BYTES = 61 * 1024 * 1024
 GRAM_BYTES = 24 * 1024 * 1024
@@ -43,7 +44,6 @@
     tw_sem, map_sem, x_sem, s1_send, s1_recv, h_send, h_recv, z_send, z_recv, t_send, t_recv,
 ):
     span = NFFT // PARTS
-    chunks = span // CHUNK
     half = 2 * 2 * 2 * n_z
     tm = lax.axis_index("tm")
     chan = lax.axis_index("chan")
@@ -66,16 +66,21 @@
         ]
 
     def load_table(c):
-        at = pl.ds(pl.multiple_of(c * CHUNK, CHUNK), CHUNK)
+        at = pl.ds(STARTS[c], CHUNKS[c])
         return pltpu.make_async_copy(tw_hbm.at[at], tw_v.at[at], tw_sem.at[c])
 
-    for part in range(PARTS):
-        for copy in load_frames(part):
-            copy.start()
-        for c in range(part * chunks, (part + 1) * chunks):
-            load_table(c).start()
+    frames = [load_frames(part) for part in range(PARTS)]
+    tables = [load_table(c) for c in range(len(CHUNKS))]
     signal_map = pltpu.make_async_copy(map_hbm, map_ref, map_sem)
-    signal_map.start()
+    loads = []
+    for c, start in enumerate(STARTS):
+        if start % span == 0:
+            loads.extend(frames[start // span])
+        loads.append(tables[c])
+    loads.append(signal_map)
+    early = 2 * TAPS + 3
+    for copy in loads[:early]:
+        copy.start()
 
     barrier = pltpu.get_barrier_semaphore()
 
@@ -86,25 +91,30 @@
 
     next_tm = (tm + 1) % n_tm
     prev_tm = (tm + n_tm - 1) % n_tm
+    far_z = sorted(range(1, n_z), key=lambda d: abs(d - n_z // 2))
+    far_tm = sorted(range(1, n_tm), key=lambda e: abs(e - n_tm // 2))
+    for d in far_z:
+        greet(tm, chan_of(group, (z + d) % n_z))
+    for e in far_tm:
+        greet((tm + e) % n_tm, chan)
+    for e in range(GROUP):
+        greet(prev_tm, chan_of((group + e) % GROUP, z))
     for e in range(1, GROUP):
         greet(tm, chan_of((group + e) % GROUP, z))
-    for e in range(GROUP):
-        greet(prev_tm, chan_of((group + e) % GROUP, z))
-    for d in range(1, n_z):
-        greet(tm, chan_of(group, (z + d) % n_z))
-    for e in range(1, n_tm):
-        greet((tm + e) % n_tm, chan)
-
-    for part in range(PARTS):
-        for copy in load_frames(part):
-            copy.wait()
-        for i in range(chunks):
-            c = part * chunks + i
-            load_table(c).wait()
-            frames = xs[part, :, :, i * CHUNK : (i + 1) * CHUNK].reshape(TAPS * 32, CHUNK)
-            table = tw_v[c * CHUNK : (c + 1) * CHUNK, :]
-            product = jnp.dot(frames, table, preferred_element_type=jnp.float32)
-            acc[...] = product if c == 0 else acc[...] + product
+
+    for copy in loads[early:]:
+        copy.start()
+
+    for c, start in enumerate(STARTS):
+        if start % span == 0:
+            for copy in frames[start // span]:
+                copy.wait()
+        tables[c].wait()
+        lanes = slice(start % span, start % span + CHUNKS[c])
+        left = xs[start // span, :, :, lanes].reshape(TAPS * 32, CHUNKS[c])
+        table = tw_v[start : start + CHUNKS[c], :]
+        product = jnp.dot(left, table, preferred_element_type=jnp.float32)
+        acc[...] = product if c == 0 else acc[...] + product
 
     def tap_sum(s, taps):
         return sum(
@@ -173,7 +183,7 @@
     tiles[...] = tiles32[...].reshape(n_z, 8, 128).astype(jnp.bfloat16)
 
     recvs = []
-    for d in sorted(range(1, n_z), key=lambda d: abs(d - n_z // 2)):
+    for d in far_z:
         to = (z + d) % n_z
         copy = pltpu.make_async_remote_copy(
             src_ref=tiles.at[to], dst_ref=ring.at[z],
@@ -198,7 +208,7 @@
     out_ref[tm] = ordered.astype(jnp.bfloat16)
 
     recvs = []
-    for e in sorted(range(1, n_tm), key=lambda e: abs(e - n_tm // 2)):
+    for e in far_tm:
         copy = pltpu.make_async_remote_copy(
             src_ref=out_ref.at[tm], dst_ref=out_ref.at[tm],
             send_sem=t_send.at[e], recv_sem=t_recv.at[e],
@@ -270,7 +280,7 @@
             pltpu.VMEM((n_z, 8, 128), bf16),
             pltpu.VMEM((n_z, 8, 128), bf16),
             pltpu.VMEM((256, signals), bf16),
-            dma((NFFT // CHUNK,)),
+            dma((len(CHUNKS),)),
             dma,
             dma((PARTS, TAPS)),
             dma((GROUP,)),
@@ -288,7 +298,7 @@
         name="turn",
     )(samples, jnp.asarray(table), input_map.reshape(1, signals))
     rows = signals // n_tm
-    width = min(256, signals)
+    width = min(512, signals)
     n_block = signals // width
     return pl.pallas_call(
         functools.partial(gram_kernel, n_tm),

time: 34.9 us -> 34.9 us (level)
  no operation moved by 1% of the time
where the time goes in v2:
time: 34.9 us; the launch traced here: 34.8 us
  Pallas kernels  34.8 us (100%)
    pallas_call x1, Pallas kernels, shards(): pl.pallas_call(functools.partial(turn_kernel, n_tm, n_z), out_shape=pltpu...  33.1 us
    pallas_call x1, Pallas kernels, shards(): pl.pallas_call(functools.partial(gram_kernel, n_tm), out_shape=jax.ShapeD...  1.72 us

profile of v2, /device:TPU:1, one launch (start us, length us, event | category | flops | bytes accessed | tf_op | source)
XLA Modules:
  0.0 34.8 jit_solution(9212314669769102568)
XLA Ops:
  0.0 33.1 %turn.1.x_ref = bf16[8,8,2048]{2,1,0:T(8,128)(2,1)S(1)} custom-call(bf16[32,32768]{1,0:T(8,128)(2,1)} %x_hbm.1, bf16[8192,512]{1,0:T(8,128)(2,1)} %constant.2.clone.tw_hbm, s32[1,2048]{1,0:T(1,128)} %bitcast.1), custom_call_target="tpu_custom_call" | custom-call | tf_op jit(solution)/shard_map/turn/pallas_call | solution.py:261
  33.1 1.7 %gram.1 = bf16[1,2,256,2048]{3,2,1,0:T(8,128)(2,1)} custom-call(bf16[8,8,2048]{2,1,0:T(8,128)(2,1)S(1)} %turn.1.x_ref), custom_call_target="tpu_custom_call" | custom-call | tf_op jit(solution)/shard_map/gram/pallas_call | solution.py:303
